TPU v7x, 32 devices: a whole 2x2x4 slice. The times are simulated.
32 devices in a mesh: grp: 2 (over x), tile: 16 (over z, y, core).
Axes of the slice: x: 2, y: 2, z: 4, core: 2. Of those that a mesh axis runs over, the one named last changes fastest.
Arguments:
- state: bfloat16 [256, 16, 512], P(('grp', 'tile')), parts along dimension 0, may hold values from -36 to 36
- wet: int32 [128], replicated, may hold values from 0 to 1, as said below
- w_vqkv: bfloat16 [512, 1536], replicated, may hold values from -0.25 to 0.25
- w_vout: bfloat16 [512, 512], replicated, may hold values from -0.25 to 0.25
- w_hqkv: bfloat16 [512, 1536], replicated, may hold values from -0.25 to 0.25
- w_hout: bfloat16 [512, 512], replicated, may hold values from -0.25 to 0.25
Outputs:
- updated: bfloat16 [256, 16, 512], P(('grp', 'tile')), parts along dimension 0
There are 2 independent parts, one for each index of `grp`. A program takes and returns all parts, laid end to end along the dimension named above; an argument that names none is the same for every part. Nothing has to cross between parts.
Inputs may be any that keep to these rules, and one draw needn't show every extreme that they name: For every strip s (blocks s * 8 to s * 8 + 7), exactly 1 of the 2 blocks with b mod 4 == 0 is wet, and exactly 1 of the 2 blocks with b mod 4 == 3.
All inputs are finite; a program needn't handle non-finite values.
Results may differ from a plain program's by a relative error of at most 0.007.
Values may be sent and summed in bfloat16 or wider, within the bound.
No kernel may reach another device: no remote copies, remote signals or barrier semaphores. Data moves between devices by JAX's collectives and lax.ppermute only.
A program may use at most 64 MiB of HBM per device.

v0:
```python
import functools
import math

import jax
import jax.numpy as jnp
from jax import lax
from jax.experimental import pallas as pl
from jax.experimental.pallas import tpu as pltpu
from jax.sharding import PartitionSpec as P

HEADS = 4
CB = 4
EPSILON = 1e-06
BF = jnp.bfloat16
F32 = jnp.float32


def each(count, body):
    if count == 1:
        body(0)
    else:
        pl.loop(0, count)(body)


def rows_at(start, size):
    if isinstance(start, int):
        return pl.ds(start, size)
    return pl.ds(pl.multiple_of(start, size), size)


def dot(left, right):
    return jnp.dot(left, right, preferred_element_type=F32)


def dot_t(left, right):
    return lax.dot_general(left, right, (((1,), (1,)), ((), ())), preferred_element_type=F32)


def head(values, index, size):
    return values[:, index * size : (index + 1) * size]


def with_ones(values):
    return jnp.concatenate([values, jnp.ones(values.shape, values.dtype)], axis=1)


def same_block(rows, levels):
    row = lax.broadcasted_iota(jnp.int32, (rows, rows), 0) // levels
    col = lax.broadcasted_iota(jnp.int32, (rows, rows), 1) // levels
    return row == col


def project(values, squares, weights, scale, size, first=0):
    joined = dot(values, weights)
    inverse = lax.rsqrt(squares)
    floor = squares * EPSILON
    out = []
    for part in range(3 * HEADS - first * HEADS):
        kind = part // HEADS + first
        piece = head(joined, part, size)
        if kind == 2:
            out.append((piece * inverse).astype(BF))
        else:
            factor = lax.rsqrt(jnp.mean(piece * piece, axis=-1, keepdims=True) + floor)
            out.append((piece * (factor * scale if kind == 0 else factor)).astype(BF))
    return [out[i : i + HEADS] for i in range(0, len(out), HEADS)]


def mean_square(values):
    return jnp.mean(values * values, axis=-1, keepdims=True) + EPSILON


def vertical_context(block, w_vqkv, levels):
    rows, width = block.shape
    size = width // HEADS
    scale = math.log2(math.e) / math.sqrt(size)
    values = block.astype(F32)
    heads = range(HEADS)
    keys = dot(block, w_vqkv[:, width : 2 * width])
    queries = dot(block, w_vqkv[:, :width])
    vals = dot(block, w_vqkv[:, 2 * width :])
    squares = mean_square(values)
    squares_k = dot_t(jnp.full((8, width), 1.0 / width, BF), (values * values).astype(BF))[0:1]
    floor, floor_k = squares * EPSILON, (squares_k + EPSILON) * EPSILON
    keys_sq = (keys * keys).astype(BF)
    queries_b, keys_b = queries.astype(BF), keys.astype(BF)
    scores = [dot_t(head(queries_b, h, size), head(keys_b, h, size)) for h in heads]
    ones = jnp.full((8, size), 1.0 / size, BF)
    means_k = [dot_t(ones, head(keys_sq, h, size))[0:1] for h in heads]
    norms_q = [
        lax.rsqrt(jnp.mean(q * q, axis=-1, keepdims=True) + floor) * scale
        for q in (head(queries, h, size) for h in heads)
    ]
    norms_k = [lax.rsqrt(m + floor_k) for m in means_k]
    vals = (vals * lax.rsqrt(squares)).astype(BF)
    expons = [jnp.exp2(x * q * k) for x, q, k in zip(scores, norms_q, norms_k)]
    if rows > levels:
        inside = same_block(rows, levels)
        expons = [jnp.where(inside, e, 0.0) for e in expons]
    totals = [dot(e.astype(BF), with_ones(head(vals, h, size))) for h, e in enumerate(expons)]
    parts = [(t[:, :size] / t[:, size:]).astype(BF) for t in totals]
    return jnp.concatenate(parts, axis=1)


def edge_kernel(wet_hbm, x_hbm, to_right, to_left, wet_ref, held, sems):
    blocks = x_hbm.shape[0] * CB
    tile = lax.axis_index("tile")
    copies = [
        pltpu.make_async_copy(wet_hbm, wet_ref, sems.at[0]),
        pltpu.make_async_copy(x_hbm.at[:, CB - 1], held.at[0], sems.at[1]),
        pltpu.make_async_copy(x_hbm.at[:, 0], held.at[1], sems.at[2]),
    ]
    for copy in copies:
        copy.start()
    for copy in copies:
        copy.wait()
    for i, (out_ref, column) in enumerate(((to_right, CB - 1), (to_left, 0))):
        out_ref[...] = jnp.where(wet_ref[0, tile * blocks + column] > 0, held[i, 0], held[i, 1])


def early_kernel(levels, *refs):
    operands, outputs = refs[:6], refs[7:12]

    def run(*scratch):
        *loaded, mixed_s, sems = scratch
        copies = [
            pltpu.make_async_copy(a, b, sems.at[i]) for i, (a, b) in enumerate(zip(operands, loaded))
        ]
        for copy in copies:
            copy.start()
        own_blocks(levels, *loaded, *outputs, mixed_s, copies)

    @pl.when(lax.axis_index("tile") == 0)
    def _():
        pl.run_scoped(
            run,
            *[pltpu.VMEM(ref.shape, ref.dtype) for ref in operands],
            pltpu.VMEM(operands[0].shape, BF),
            pltpu.SemaphoreType.DMA((len(operands),)),
        )


def late_kernel(levels, *refs):
    @pl.when(lax.axis_index("tile") != 0)
    def _():
        own_blocks(levels, *refs[:6], *refs[11:16], refs[16], ())


def own_blocks(
    levels, x_ref, w_vqkv, w_vout, wet_ref, w_hqkv, w_hout,
    result_ref, base_e, query_e, term_e, den_e, mixed_s, copies,
):
    total_rows, width = x_ref.shape
    size = width // HEADS
    scale = math.log2(math.e) / math.sqrt(size)
    blocks = total_rows // levels
    chunk = min(levels, 16)
    edges = [b for b in range(blocks) if b % CB in (0, CB - 1)]
    tile = lax.axis_index("tile")
    group = min(max(levels, 128), total_rows)

    def mix(index):
        rows = rows_at(index * group, group)
        block = x_ref[rows, :]
        context = vertical_context(block, w_vqkv, levels)
        mixed_s[rows, :] = (block.astype(F32) + dot(context, w_vout[...])).astype(BF)

    for copy in copies[:3]:
        copy.wait()
    each(total_rows // group, mix)
    for copy in copies[3:]:
        copy.wait()

    rows = blocks * chunk
    row = lax.broadcasted_iota(jnp.int32, (rows, rows), 0)
    col = lax.broadcasted_iota(jnp.int32, (rows, rows), 1)
    block_q, block_k = row // chunk, col // chunk
    wet = jnp.broadcast_to(wet_ref[...], (8, wet_ref.shape[1])).astype(BF)
    which = lax.broadcasted_iota(jnp.int32, (wet.shape[1], rows), 0)
    column = lax.broadcasted_iota(jnp.int32, (wet.shape[1], rows), 1) // chunk
    wet_k = dot(wet, (which == tile * blocks + column).astype(BF))[0:1, :]
    near = jnp.abs(block_q % CB - block_k % CB) <= 1
    near = near & (jnp.abs(block_q // CB - block_k // CB) <= 1)
    allowed = (row % chunk == col % chunk) & ((block_q == block_k) | (near & (wet_k > 0.5)))

    def attend(index):
        def spots(b):
            return rows_at(b * levels + index * chunk, chunk)

        mixed = jnp.concatenate([mixed_s[spots(b), :] for b in range(blocks)], axis=0)
        values = mixed.astype(F32)
        queries, keys, vals = project(mixed, mean_square(values), w_hqkv[...], scale, size)
        expons = [jnp.exp2(dot_t(q, k)) for q, k in zip(queries, keys)]
        expons = [jnp.where(allowed, e, 0.0).astype(BF) for e in expons]
        totals = [dot(e, with_ones(v)) for e, v in zip(expons, vals)]
        parts = [(t[:, :size] / t[:, size:]).astype(BF) for t in totals]
        inner = [b for b in range(blocks) if b not in edges]

        def some(array, which):
            return jnp.concatenate([array[b * chunk : (b + 1) * chunk] for b in which], axis=0)

        context = jnp.concatenate([some(p, inner) for p in parts], axis=1)
        result = (some(values, inner) + dot(context, w_hout[...])).astype(BF)
        terms = [
            dot(some(p, edges), w_hout[h * size : (h + 1) * size, :]) for h, p in enumerate(parts)
        ]
        base = some(values, edges) + sum(terms)
        for i, b in enumerate(inner):
            result_ref[spots(b), :] = result[i * chunk : (i + 1) * chunk]
        for e, b in enumerate(edges):
            here = slice(e * chunk, (e + 1) * chunk)
            there = rows_at(e * levels + index * chunk, chunk)
            base_e[there, :] = base[here]
            for h in range(HEADS):
                cols = slice(h * size, (h + 1) * size)
                query_e[there, cols] = queries[h][b * chunk : (b + 1) * chunk].astype(F32)
                den_e[there, cols] = totals[h][b * chunk : (b + 1) * chunk, size:]
                term_e[h, there, :] = terms[h][here]

    each(levels // chunk, attend)


def halo_kernel(
    levels, blocks, from_left, from_right, base_e, query_e, term_e, den_e,
    w_vqkv, w_vout, w_hqkv, w_hout, inner_ref, out_ref, result_s, sem,
):
    width = base_e.shape[1]
    size = width // HEADS
    chunk = min(levels, 16)
    edges = [b for b in range(blocks) if b % CB in (0, CB - 1)]
    group = 2 * levels if 2 * levels <= 128 else levels
    for b in range(blocks):
        if b not in edges:
            here = pl.ds(b * levels, levels)
            result_s[here, :] = inner_ref[here, :]

    halo = jnp.concatenate([from_left[...], from_right[...]], axis=0)
    heads = range(HEADS)
    pieces = []
    for start in range(0, 2 * levels, group):
        block = halo[start : start + group]
        context = vertical_context(block, w_vqkv, levels)
        mixed = (block.astype(F32) + dot(context, w_vout[...])).astype(BF)
        joined = dot(mixed, w_hqkv[:, width:])
        mixed = mixed.astype(F32)
        squares = mean_square(mixed)
        values = (joined[:, width:] * lax.rsqrt(squares)).astype(BF)
        moved = [
            dot(head(values, h, size), w_hout[h * size : (h + 1) * size, :]) for h in heads
        ]
        pieces.append((joined[:, :width], squares * EPSILON, *moved))
    keys, floor, *moved = (jnp.concatenate(p, axis=0) for p in zip(*pieces))

    for index in range(levels // chunk):
        def take(source, count):
            return jnp.concatenate(
                [source[i * levels + index * chunk :][:chunk] for i in range(count)], axis=0
            )

        def per_edge(values):
            sides = [values[:chunk], values[chunk:]]
            return jnp.concatenate([sides[0 if b % CB == 0 else 1] for b in edges], axis=0)

        def edge(*spot):
            return jnp.concatenate(
                [
                    ref[(*lead, pl.ds(e * levels + index * chunk, chunk), slice(None))]
                    for ref, *lead in [spot]
                    for e in range(len(edges))
                ],
                axis=0,
            )

        chunk_keys, chunk_floor = take(keys, 2), take(floor, 2)
        product = edge(query_e) * per_edge(chunk_keys)
        squares = chunk_keys * chunk_keys
        scores = [jnp.sum(head(product, h, size), axis=-1, keepdims=True) for h in heads]
        means = [jnp.mean(head(squares, h, size), axis=-1, keepdims=True) for h in heads]
        norms = [per_edge(lax.rsqrt(m + chunk_floor)) for m in means]
        expons = [jnp.exp2(x * n) for x, n in zip(scores, norms)]
        den = edge(den_e)
        shares = [e / (den[:, h * size : h * size + 1] + e) for h, e in enumerate(expons)]
        result = edge(base_e)
        for h, share in enumerate(shares):
            result = result + share * (per_edge(take(moved[h], 2)) - edge(term_e, h))
        result = result.astype(BF)
        for e, b in enumerate(edges):
            there = pl.ds(b * levels + index * chunk, chunk)
            result_s[there, :] = result[e * chunk : (e + 1) * chunk]

    copy = pltpu.make_async_copy(result_s, out_ref, sem)
    copy.start()
    copy.wait()


def on_device(state, wet, w_vqkv, w_vout, w_hqkv, w_hout):
    tiles = lax.axis_size("tile")
    blocks, levels, width = state.shape
    rows = blocks // CB
    edge_rows = 2 * rows * levels
    limit = (10 << 20) + levels * (256 << 10)
    vmem = pl.BlockSpec(memory_space=pltpu.VMEM)
    hbm = pl.BlockSpec(memory_space=pl.ANY)
    whole = jax.ShapeDtypeStruct((blocks * levels, width), BF)
    strip = state.reshape(rows, CB, levels, width)
    one = jax.ShapeDtypeStruct((levels, width), BF)
    to_right, to_left = pl.pallas_call(
        edge_kernel,
        out_shape=(one, one),
        in_specs=[hbm] * 2,
        out_specs=(vmem,) * 2,
        scratch_shapes=[
            pltpu.SMEM((1, wet.shape[0]), wet.dtype),
            pltpu.VMEM((2, rows, levels, width), BF),
            pltpu.SemaphoreType.DMA((3,)),
        ],
        compiler_params=pltpu.CompilerParams(vmem_limit_bytes=4 << 20),
        cost_estimate=pl.CostEstimate(flops=200 << 30, bytes_accessed=1 << 30, transcendentals=0),
        name="edge_blocks",
    )(*[pltpu.with_memory_space_constraint(v, pltpu.HBM) for v in (wet.reshape(1, -1), strip)])
    from_left = lax.ppermute(to_right, "tile", [(i, (i + 1) % tiles) for i in range(tiles)])
    edge_f32 = jax.ShapeDtypeStruct((edge_rows, width), F32)
    results = (
        whole,
        edge_f32,
        edge_f32,
        jax.ShapeDtypeStruct((HEADS, edge_rows, width), F32),
        edge_f32,
    )
    operands = (
        state.reshape(blocks * levels, width), w_vqkv, w_vout, wet.reshape(1, -1), w_hqkv, w_hout
    )
    mixed_s = pltpu.VMEM((blocks * levels, width), BF)
    cost = pl.CostEstimate(
        flops=2 * blocks * levels * width * width * 8, bytes_accessed=8 << 20, transcendentals=0
    )
    *early, to_left = pl.pallas_call(
        functools.partial(early_kernel, levels),
        out_shape=results + (jax.ShapeDtypeStruct(to_left.shape, to_left.dtype),),
        in_specs=[hbm] * 6 + [vmem],
        out_specs=(vmem,) * 6,
        input_output_aliases={6: 5},
        compiler_params=pltpu.CompilerParams(vmem_limit_bytes=limit + (6 << 20)),
        cost_estimate=cost,
        name="early_blocks",
    )(*[pltpu.with_memory_space_constraint(v, pltpu.HBM) for v in operands], to_left)
    from_right = lax.ppermute(to_left, "tile", [(i, (i - 1) % tiles) for i in range(tiles)])

    inner, *edge_values = pl.pallas_call(
        functools.partial(late_kernel, levels),
        out_shape=results,
        in_specs=[vmem] * 11,
        out_specs=(vmem,) * 5,
        input_output_aliases={6 + i: i for i in range(5)},
        scratch_shapes=[mixed_s],
        compiler_params=pltpu.CompilerParams(vmem_limit_bytes=limit),
        cost_estimate=cost,
        name="late_blocks",
    )(*operands, *early)
    updated = pl.pallas_call(
        functools.partial(halo_kernel, levels, blocks),
        out_shape=whole,
        in_specs=[vmem] * 11,
        out_specs=hbm,
        scratch_shapes=[
            pltpu.VMEM(whole.shape, BF),
            pltpu.SemaphoreType.DMA,
        ],
        compiler_params=pltpu.CompilerParams(vmem_limit_bytes=limit),
        name="halo_blocks",
    )(from_left, from_right, *edge_values, w_vqkv, w_vout, w_hqkv, w_hout, inner)
    return updated.reshape(blocks, levels, width)


def solution(mesh):
    in_specs = (P(("grp", "tile"), None, None), P(), P(), P(), P(), P())
    out_specs = P(("grp", "tile"), None, None)
    return jax.shard_map(
        on_device, mesh=mesh, in_specs=in_specs, out_specs=out_specs, check_vma=False
    )
```

profile of v0, /device:TPU:0, one launch (start us, length us, event | category | flops | bytes accessed | tf_op | source)
XLA Modules:
  0.0 9.8 jit_solution(496979976638680483)
XLA Ops:
  0.0 0.8 %edge_blocks.1 = (bf16[16,512]{1,0:T(8,128)(2,1)S(1)}, bf16[16,512]{1,0:T(8,128)(2,1)S(1)}) custom-call(s32[1,128]{1,0:T(1,128)} %bitcast.7, bf16[2,4,16,512]{3,2,1,0:T(8,128)(2,1)} %bitcast.4), custom_call_target="tpu_custom_call" | custom-call | flops 214748364800 | bytes 1073741824 | tf_op jit(solution)/shard_map/edge_blocks/pallas_call | solution.py:307
  0.8 0.5 %collective-permute-start = (bf16[16,512]{1,0:T(8,128)(2,1)S(1)}, bf16[16,512]{1,0:T(8,128)(2,1)S(1)}, u32[]{:S(2)}, u32[]{:S(2)}) collective-permute-start(bf16[16,512]{1,0:T(8,128)(2,1)S(1)} %get-tuple-element.18), channel_id=1, source_target_pairs={{0,1},{1,2},{2,3},{3,4},{4,5},{5,6},{6,7},{7,8},{8,9},{9,10},{10,1... | collective-permute-start | bytes 49160 | tf_op jit(solution)/shard_map/ppermute | solution.py:321
  1.3 0.0 copy-start
  1.3 0.0 copy-start.1
  1.3 0.0 copy-start.2
  1.3 0.0 copy-start.3
  1.3 0.0 copy-start.4
  1.3 0.0 copy-start.5
  1.4 3.6 %early_blocks.1 = (bf16[128,512]{1,0:T(8,128)(2,1)S(1)}, f32[64,512]{1,0:T(8,128)S(1)}, f32[64,512]{1,0:T(8,128)S(1)}, f32[4,64,512]{2,1,0:T(8,128)S(1)}, f32[64...) custom-call(bf16[128,512]{1,0:T(8,128)(2,1)} %bitcast.5, ...), custom_call_target="tpu_custom_call", output_to_operand_aliasing={{5}: (6, {})} | custom-call | flops 536870912 | bytes 8388608 | tf_op jit(solution)/shard_map/early_blocks/pallas_call | solution.py:337
  4.9 1.5 %collective-permute-start.1 = (bf16[16,512]{1,0:T(8,128)(2,1)S(1)}, bf16[16,512]{1,0:T(8,128)(2,1)S(1)}, u32[]{:S(2)}, u32[]{:S(2)}) collective-permute-start(bf16[16,512]{1,0:T(8,128)(2,1)S(1)} %get-tuple-element.20), channel_id=1, source_target_pairs={{0,15},{1,0},{2,1},{3,2},{4,3},{5,4},{6,5},{7,6},{8,7},{9,8},{10,9... | collective-permute-start | bytes 49160 | tf_op jit(solution)/shard_map/ppermute | solution.py:347
  6.5 0.0 copy-done
  6.5 0.0 copy-done.1
  6.5 0.0 copy-done.2
  6.5 0.0 copy-done.3
  6.5 0.0 copy-done.4
  6.5 0.0 copy-done.5
  6.5 1.2 %collective-permute-done.from_left = bf16[16,512]{1,0:T(8,128)(2,1)S(1)} collective-permute-done((bf16[16,512]{1,0:T(8,128)(2,1)S(1)}, bf16[16,512]{1,0:T(8,128)(2,1)S(1)}, u32[]{:S(2)}, u32[]{:S(2)}) %collective-permute-start) | collective-permute-done | bytes 16416 | tf_op jit(solution)/shard_map/ppermute | solution.py:321
  7.7 0.2 %collective-permute-done.1.from_right = bf16[16,512]{1,0:T(8,128)(2,1)S(1)} collective-permute-done((bf16[16,512]{1,0:T(8,128)(2,1)S(1)}, bf16[16,512]{1,0:T(8,128)(2,1)S(1)}, u32[]{:S(2)}, u32[]{:S(2)}) %collective-permute-start.1) | collective-permute-done | bytes 16416 | tf_op jit(solution)/shard_map/ppermute | solution.py:347
  7.9 1.8 %halo_blocks.1 = bf16[128,512]{1,0:T(8,128)(2,1)} custom-call(bf16[16,512]{1,0:T(8,128)(2,1)S(1)} %collective-permute-done.from_left, bf16[16,512]{1,0:T(8,128)(2,1)S(1)} %collective-permute-done.1.from_right, f32[64,512]{1,0:T(8,128)S(1)} %get-tuple-element.26.base_e, f32[64,512]{1,0:T(8,128)S(1)} %get-tuple-element.27.query_e, ...), custom_call_target="tpu_custom_call" | custom-call | tf_op jit(solution)/shard_map/halo_blocks/pallas_call | solution.py:360
  (1 shorter events, 0.0 us)
Async XLA Ops:
  0.8 6.9 %collective-permute-start = (bf16[16,512]{1,0:T(8,128)(2,1)S(1)}, bf16[16,512]{1,0:T(8,128)(2,1)S(1)}, u32[]{:S(2)}, u32[]{:S(2)}) collective-permute-start(bf16[16,512]{1,0:T(8,128)(2,1)S(1)} %get-tuple-element.18), channel_id=1, source_target_pairs={{0,1},{1,2},{2,3},{3,4},{4,5},{5,6},{6,7},{7,8},{8,9},{9,10},{10,1... | collective-permute-start | bytes 49160 | tf_op jit(solution)/shard_map/ppermute | solution.py:321
  1.3 5.2 %copy-start = (bf16[512,1536]{1,0:T(8,128)(2,1)S(1)}, bf16[512,1536]{1,0:T(8,128)(2,1)}, u32[]{:S(2)}) copy-start(bf16[512,1536]{1,0:T(8,128)(2,1)} %w_vqkv.1) | copy-start | bytes 4718596
  1.3 5.2 %copy-start.1 = (bf16[512,1536]{1,0:T(8,128)(2,1)S(1)}, bf16[512,1536]{1,0:T(8,128)(2,1)}, u32[]{:S(2)}) copy-start(bf16[512,1536]{1,0:T(8,128)(2,1)} %w_hqkv.1) | copy-start | bytes 4718596
  1.3 5.2 %copy-start.2 = (bf16[512,512]{1,0:T(8,128)(2,1)S(1)}, bf16[512,512]{1,0:T(8,128)(2,1)}, u32[]{:S(2)}) copy-start(bf16[512,512]{1,0:T(8,128)(2,1)} %w_vout.1) | copy-start | bytes 1572868
  1.3 5.2 %copy-start.3 = (bf16[512,512]{1,0:T(8,128)(2,1)S(1)}, bf16[512,512]{1,0:T(8,128)(2,1)}, u32[]{:S(2)}) copy-start(bf16[512,512]{1,0:T(8,128)(2,1)} %w_hout.1) | copy-start | bytes 1572868
  1.3 5.2 %copy-start.4 = (bf16[8,16,512]{2,1,0:T(8,128)(2,1)S(1)}, bf16[8,16,512]{2,1,0:T(8,128)(2,1)}, u32[]{:S(2)}) copy-start(bf16[8,16,512]{2,1,0:T(8,128)(2,1)} %param.6) | copy-start | bytes 393220
  1.3 5.2 %copy-start.5 = (s32[128]{0:T(128)S(1)}, s32[128]{0:T(128)}, u32[]{:S(2)}) copy-start(s32[128]{0:T(128)} %param.7) | copy-start | bytes 1540
  4.9 3.0 %collective-permute-start.1 = (bf16[16,512]{1,0:T(8,128)(2,1)S(1)}, bf16[16,512]{1,0:T(8,128)(2,1)S(1)}, u32[]{:S(2)}, u32[]{:S(2)}) collective-permute-start(bf16[16,512]{1,0:T(8,128)(2,1)S(1)} %get-tuple-element.20), channel_id=1, source_target_pairs={{0,15},{1,0},{2,1},{3,2},{4,3},{5,4},{6,5},{7,6},{8,7},{9,8},{10,9... | collective-permute-start | bytes 49160 | tf_op jit(solution)/shard_map/ppermute | solution.py:347
where the time goes:
time: 9.94 us; the launch traced here: 9.76 us
  Pallas kernels  6.24 us (63%)
  starting transfers between devices  2.04 us (21%)
  waiting for transfers between devices  1.39 us (14%)
    pallas_call x1, Pallas kernels, on_device(): pl.pallas_call(functools.partial(early_kernel, levels), out_shape=results...  3.58 us
    pallas_call x1, Pallas kernels, on_device(): pl.pallas_call(functools.partial(halo_kernel, levels, blocks), out_shape=...  1.85 us
    ppermute x1, starting transfers between devices, on_device(): lax.ppermute(to_left, 'tile', [(i, (i - 1) % tiles) for i in range(tiles)])  1.53 us
    ppermute x1, waiting for transfers between devices, on_device(): lax.ppermute(to_right, 'tile', [(i, (i + 1) % tiles) for i in range(tiles)])  1.2 us
    pallas_call x1, Pallas kernels, on_device(): pl.pallas_call(edge_kernel, out_shape=(one, one), in_specs=[hbm] * 2, out...  0.81 us
    ppermute x1, starting transfers between devices, on_device(): lax.ppermute(to_right, 'tile', [(i, (i + 1) % tiles) for i in range(tiles)])  0.5 us
  transfers between devices with their start and end apart: 2, of which 2 were waited for; matrix products, arithmetic and copies ran while one was open for 0% of the time, Pallas kernels for 37%

commit v1 on v0

--- a/solution.py
+++ b/solution.py
@@ -120,6 +120,7 @@
 
 def early_kernel(levels, *refs):
     operands, outputs = refs[:6], refs[7:12]
+    refs[12][...] = refs[6][...]
 
     def run(*scratch):
         *loaded, mixed_s, sems = scratch
@@ -141,9 +142,16 @@
 
 
 def late_kernel(levels, *refs):
+    operands, early, outputs, mixed_s = refs[:6], refs[6:11], refs[11:16], refs[16]
+
+    @pl.when(lax.axis_index("tile") == 0)
+    def _():
+        for source, target in zip(early, outputs):
+            target[...] = source[...]
+
     @pl.when(lax.axis_index("tile") != 0)
     def _():
-        own_blocks(levels, *refs[:6], *refs[11:16], refs[16], ())
+        own_blocks(levels, *operands, *outputs, mixed_s, ())
 
 
 def own_blocks(
@@ -339,7 +347,6 @@
         out_shape=results + (jax.ShapeDtypeStruct(to_left.shape, to_left.dtype),),
         in_specs=[hbm] * 6 + [vmem],
         out_specs=(vmem,) * 6,
-        input_output_aliases={6: 5},
         compiler_params=pltpu.CompilerParams(vmem_limit_bytes=limit + (6 << 20)),
         cost_estimate=cost,
         name="early_blocks",
@@ -351,7 +358,6 @@
         out_shape=results,
         in_specs=[vmem] * 11,
         out_specs=(vmem,) * 5,
-        input_output_aliases={6 + i: i for i in range(5)},
         scratch_shapes=[mixed_s],
         compiler_params=pltpu.CompilerParams(vmem_limit_bytes=limit),
         cost_estimate=cost,

time: 9.94 us -> 9.95 us (level)
  no operation moved by 1% of the time
where the time goes in v1:
time: 9.95 us; the launch traced here: 9.78 us
  Pallas kernels  6.32 us (64%)
  starting transfers between devices  2.04 us (21%)
  waiting for transfers between devices  1.32 us (13%)
    pallas_call x1, Pallas kernels, on_device(): pl.pallas_call(functools.partial(early_kernel, levels), out_shape=results...  3.58 us
    pallas_call x1, Pallas kernels, on_device(): pl.pallas_call(functools.partial(halo_kernel, levels, blocks), out_shape=...  1.86 us
    ppermute x1, starting transfers between devices, on_device(): lax.ppermute(to_left, 'tile', [(i, (i - 1) % tiles) for i in range(tiles)])  1.53 us
    ppermute x1, waiting for transfers between devices, on_device(): lax.ppermute(to_right, 'tile', [(i, (i + 1) % tiles) for i in range(tiles)])  1.14 us
    pallas_call x1, Pallas kernels, on_device(): pl.pallas_call(edge_kernel, out_shape=(one, one), in_specs=[hbm] * 2, out...  0.81 us
    ppermute x1, starting transfers between devices, on_device(): lax.ppermute(to_right, 'tile', [(i, (i + 1) % tiles) for i in range(tiles)])  0.5 us
  transfers between devices with their start and end apart: 2, of which 2 were waited for; matrix products, arithmetic and copies ran while one was open for 0% of the time, Pallas kernels for 37%

profile of v1, /device:TPU:0, one launch (start us, length us, event | category | flops | bytes accessed | tf_op | source)
XLA Modules:
  0.0 9.8 jit_solution(7918534730754225024)
XLA Ops:
  0.0 0.8 %edge_blocks.1 = (bf16[16,512]{1,0:T(8,128)(2,1)S(1)}, bf16[16,512]{1,0:T(8,128)(2,1)S(1)}) custom-call(s32[1,128]{1,0:T(1,128)} %bitcast.7, bf16[2,4,16,512]{3,2,1,0:T(8,128)(2,1)} %bitcast.4), custom_call_target="tpu_custom_call" | custom-call | flops 214748364800 | bytes 1073741824 | tf_op jit(solution)/shard_map/edge_blocks/pallas_call | solution.py:315
  0.8 0.5 %collective-permute-start = (bf16[16,512]{1,0:T(8,128)(2,1)S(1)}, bf16[16,512]{1,0:T(8,128)(2,1)S(1)}, u32[]{:S(2)}, u32[]{:S(2)}) collective-permute-start(bf16[16,512]{1,0:T(8,128)(2,1)S(1)} %get-tuple-element.18), channel_id=1, source_target_pairs={{0,1},{1,2},{2,3},{3,4},{4,5},{5,6},{6,7},{7,8},{8,9},{9,10},{10,1... | collective-permute-start | bytes 49160 | tf_op jit(solution)/shard_map/ppermute | solution.py:329
  1.3 0.0 copy-start
  1.3 0.0 copy-start.1
  1.3 0.0 copy-start.2
  1.3 0.0 copy-start.3
  1.3 0.0 copy-start.4
  1.3 0.0 copy-start.5
  1.4 3.6 %early_blocks.1 = (bf16[128,512]{1,0:T(8,128)(2,1)S(1)}, f32[64,512]{1,0:T(8,128)S(1)}, f32[64,512]{1,0:T(8,128)S(1)}, f32[4,64,512]{2,1,0:T(8,128)S(1)}, f32[64...) custom-call(bf16[128,512]{1,0:T(8,128)(2,1)} %bitcast.5, bf16[512,1536]{1,0:T(8,128)(2,1)} %w_vqkv.1, ...), custom_call_target="tpu_custom_call" | custom-call | flops 536870912 | bytes 8388608 | tf_op jit(solution)/shard_map/early_blocks/pallas_call | solution.py:345
  4.9 1.5 %collective-permute-start.1 = (bf16[16,512]{1,0:T(8,128)(2,1)S(1)}, bf16[16,512]{1,0:T(8,128)(2,1)S(1)}, u32[]{:S(2)}, u32[]{:S(2)}) collective-permute-start(bf16[16,512]{1,0:T(8,128)(2,1)S(1)} %get-tuple-element.20), channel_id=1, source_target_pairs={{0,15},{1,0},{2,1},{3,2},{4,3},{5,4},{6,5},{7,6},{8,7},{9,8},{10,9... | collective-permute-start | bytes 49160 | tf_op jit(solution)/shard_map/ppermute | solution.py:354
  6.5 0.0 copy-done
  6.5 0.0 copy-done.1
  6.5 0.0 copy-done.2
  6.5 0.0 copy-done.3
  6.5 0.0 copy-done.4
  6.5 0.0 copy-done.5
  6.5 0.1 late_blocks.1
  6.6 1.1 %collective-permute-done.from_left = bf16[16,512]{1,0:T(8,128)(2,1)S(1)} collective-permute-done((bf16[16,512]{1,0:T(8,128)(2,1)S(1)}, bf16[16,512]{1,0:T(8,128)(2,1)S(1)}, u32[]{:S(2)}, u32[]{:S(2)}) %collective-permute-start) | collective-permute-done | bytes 16416 | tf_op jit(solution)/shard_map/ppermute | solution.py:329
  7.7 0.2 %collective-permute-done.1.from_right = bf16[16,512]{1,0:T(8,128)(2,1)S(1)} collective-permute-done((bf16[16,512]{1,0:T(8,128)(2,1)S(1)}, bf16[16,512]{1,0:T(8,128)(2,1)S(1)}, u32[]{:S(2)}, u32[]{:S(2)}) %collective-permute-start.1) | collective-permute-done | bytes 16416 | tf_op jit(solution)/shard_map/ppermute | solution.py:354
  7.9 1.9 %halo_blocks.1 = bf16[128,512]{1,0:T(8,128)(2,1)} custom-call(bf16[16,512]{1,0:T(8,128)(2,1)S(1)} %collective-permute-done.from_left, bf16[16,512]{1,0:T(8,128)(2,1)S(1)} %collective-permute-done.1.from_right, f32[64,512]{1,0:T(8,128)S(1)} %get-tuple-element.26.base_e, f32[64,512]{1,0:T(8,128)S(1)} %get-tuple-element.27.query_e, ...), custom_call_target="tpu_custom_call" | custom-call | tf_op jit(solution)/shard_map/halo_blocks/pallas_call | solution.py:366
Async XLA Ops:
  0.8 6.9 %collective-permute-start = (bf16[16,512]{1,0:T(8,128)(2,1)S(1)}, bf16[16,512]{1,0:T(8,128)(2,1)S(1)}, u32[]{:S(2)}, u32[]{:S(2)}) collective-permute-start(bf16[16,512]{1,0:T(8,128)(2,1)S(1)} %get-tuple-element.18), channel_id=1, source_target_pairs={{0,1},{1,2},{2,3},{3,4},{4,5},{5,6},{6,7},{7,8},{8,9},{9,10},{10,1... | collective-permute-start | bytes 49160 | tf_op jit(solution)/shard_map/ppermute | solution.py:329
  1.3 5.2 %copy-start = (bf16[512,1536]{1,0:T(8,128)(2,1)S(1)}, bf16[512,1536]{1,0:T(8,128)(2,1)}, u32[]{:S(2)}) copy-start(bf16[512,1536]{1,0:T(8,128)(2,1)} %w_vqkv.1) | copy-start | bytes 4718596
  1.3 5.2 %copy-start.1 = (bf16[512,1536]{1,0:T(8,128)(2,1)S(1)}, bf16[512,1536]{1,0:T(8,128)(2,1)}, u32[]{:S(2)}) copy-start(bf16[512,1536]{1,0:T(8,128)(2,1)} %w_hqkv.1) | copy-start | bytes 4718596
  1.3 5.2 %copy-start.2 = (bf16[512,512]{1,0:T(8,128)(2,1)S(1)}, bf16[512,512]{1,0:T(8,128)(2,1)}, u32[]{:S(2)}) copy-start(bf16[512,512]{1,0:T(8,128)(2,1)} %w_vout.1) | copy-start | bytes 1572868
  1.3 5.2 %copy-start.3 = (bf16[512,512]{1,0:T(8,128)(2,1)S(1)}, bf16[512,512]{1,0:T(8,128)(2,1)}, u32[]{:S(2)}) copy-start(bf16[512,512]{1,0:T(8,128)(2,1)} %w_hout.1) | copy-start | bytes 1572868
  1.3 5.2 %copy-start.4 = (bf16[8,16,512]{2,1,0:T(8,128)(2,1)S(1)}, bf16[8,16,512]{2,1,0:T(8,128)(2,1)}, u32[]{:S(2)}) copy-start(bf16[8,16,512]{2,1,0:T(8,128)(2,1)} %param.6) | copy-start | bytes 393220
  1.3 5.2 %copy-start.5 = (s32[128]{0:T(128)S(1)}, s32[128]{0:T(128)}, u32[]{:S(2)}) copy-start(s32[128]{0:T(128)} %param.7) | copy-start | bytes 1540
  4.9 3.0 %collective-permute-start.1 = (bf16[16,512]{1,0:T(8,128)(2,1)S(1)}, bf16[16,512]{1,0:T(8,128)(2,1)S(1)}, u32[]{:S(2)}, u32[]{:S(2)}) collective-permute-start(bf16[16,512]{1,0:T(8,128)(2,1)S(1)} %get-tuple-element.20), channel_id=1, source_target_pairs={{0,15},{1,0},{2,1},{3,2},{4,3},{5,4},{6,5},{7,6},{8,7},{9,8},{10,9... | collective-permute-start | bytes 49160 | tf_op jit(solution)/shard_map/ppermute | solution.py:354

commit v2 on v1

--- a/solution.py
+++ b/solution.py
@@ -44,33 +44,50 @@
     return jnp.concatenate([values, jnp.ones(values.shape, values.dtype)], axis=1)
 
 
+def mean_square(values):
+    return jnp.mean(values * values, axis=-1, keepdims=True) + EPSILON
+
+
 def same_block(rows, levels):
     row = lax.broadcasted_iota(jnp.int32, (rows, rows), 0) // levels
     col = lax.broadcasted_iota(jnp.int32, (rows, rows), 1) // levels
     return row == col
 
 
-def project(values, squares, weights, scale, size, first=0):
-    joined = dot(values, weights)
-    inverse = lax.rsqrt(squares)
-    floor = squares * EPSILON
-    out = []
-    for part in range(3 * HEADS - first * HEADS):
-        kind = part // HEADS + first
-        piece = head(joined, part, size)
-        if kind == 2:
-            out.append((piece * inverse).astype(BF))
-        else:
-            factor = lax.rsqrt(jnp.mean(piece * piece, axis=-1, keepdims=True) + floor)
-            out.append((piece * (factor * scale if kind == 0 else factor)).astype(BF))
-    return [out[i : i + HEADS] for i in range(0, len(out), HEADS)]
-
-
-def mean_square(values):
-    return jnp.mean(values * values, axis=-1, keepdims=True) + EPSILON
+def rms_normed(values):
+    mean = jnp.mean(values * values, axis=-1, keepdims=True)
+    return (values * lax.rsqrt(mean + EPSILON)).astype(BF)
+
+
+def normed_heads(joined, size):
+    return [rms_normed(head(joined, h, size)) for h in range(HEADS)]
+
+
+def attention(queries, keys, values, allowed):
+    size = queries[0].shape[1]
+    scale = math.log2(math.e) / math.sqrt(size)
+    scores = [dot_t(q, k) for q, k in zip(queries, keys)]
+    expons = [jnp.exp2(x * scale) for x in scores]
+    if allowed is not None:
+        expons = [jnp.where(allowed, e, 0.0) for e in expons]
+    totals = [jnp.sum(e, axis=-1, keepdims=True) for e in expons]
+    probs = [(e / t).astype(BF) for e, t in zip(expons, totals)]
+    contexts = [dot(p, head(values, h, size)).astype(BF) for h, p in enumerate(probs)]
+    return contexts, totals
 
 
 def vertical_context(block, w_vqkv, levels):
+    rows, width = block.shape
+    size = width // HEADS
+    normed = rms_normed(block.astype(F32))
+    keys = normed_heads(dot(normed, w_vqkv[:, width : 2 * width]), size)
+    queries = normed_heads(dot(normed, w_vqkv[:, :width]), size)
+    values = dot(normed, w_vqkv[:, 2 * width :]).astype(BF)
+    allowed = same_block(rows, levels) if rows > levels else None
+    return jnp.concatenate(attention(queries, keys, values, allowed)[0], axis=1)
+
+
+def halo_context(block, w_vqkv, levels):
     rows, width = block.shape
     size = width // HEADS
     scale = math.log2(math.e) / math.sqrt(size)
@@ -160,7 +177,6 @@
 ):
     total_rows, width = x_ref.shape
     size = width // HEADS
-    scale = math.log2(math.e) / math.sqrt(size)
     blocks = total_rows // levels
     chunk = min(levels, 16)
     edges = [b for b in range(blocks) if b % CB in (0, CB - 1)]
@@ -197,11 +213,10 @@
 
         mixed = jnp.concatenate([mixed_s[spots(b), :] for b in range(blocks)], axis=0)
         values = mixed.astype(F32)
-        queries, keys, vals = project(mixed, mean_square(values), w_hqkv[...], scale, size)
-        expons = [jnp.exp2(dot_t(q, k)) for q, k in zip(queries, keys)]
-        expons = [jnp.where(allowed, e, 0.0).astype(BF) for e in expons]
-        totals = [dot(e, with_ones(v)) for e, v in zip(expons, vals)]
-        parts = [(t[:, :size] / t[:, size:]).astype(BF) for t in totals]
+        joined = dot(rms_normed(values), w_hqkv[...])
+        queries = normed_heads(joined[:, :width], size)
+        keys = normed_heads(joined[:, width : 2 * width], size)
+        parts, totals = attention(queries, keys, joined[:, 2 * width :].astype(BF), allowed)
         inner = [b for b in range(blocks) if b not in edges]
 
         def some(array, which):
@@ -222,7 +237,9 @@
             for h in range(HEADS):
                 cols = slice(h * size, (h + 1) * size)
                 query_e[there, cols] = queries[h][b * chunk : (b + 1) * chunk].astype(F32)
-                den_e[there, cols] = totals[h][b * chunk : (b + 1) * chunk, size:]
+                den_e[there, cols] = jnp.broadcast_to(
+                    totals[h][b * chunk : (b + 1) * chunk], (chunk, size)
+                )
                 term_e[h, there, :] = terms[h][here]
 
     each(levels // chunk, attend)
@@ -230,10 +247,11 @@
 
 def halo_kernel(
     levels, blocks, from_left, from_right, base_e, query_e, term_e, den_e,
-    w_vqkv, w_vout, w_hqkv, w_hout, inner_ref, out_ref, result_s, sem,
+    w_vqkv, w_vout, w_hqkv, w_hout, inner_ref, result_s,
 ):
     width = base_e.shape[1]
     size = width // HEADS
+    scale = math.log2(math.e) / math.sqrt(size)
     chunk = min(levels, 16)
     edges = [b for b in range(blocks) if b % CB in (0, CB - 1)]
     group = 2 * levels if 2 * levels <= 128 else levels
@@ -247,15 +265,21 @@
     pieces = []
     for start in range(0, 2 * levels, group):
         block = halo[start : start + group]
-        context = vertical_context(block, w_vqkv, levels)
+        context = halo_context(block, w_vqkv, levels)
         mixed = (block.astype(F32) + dot(context, w_vout[...])).astype(BF)
         joined = dot(mixed, w_hqkv[:, width:])
         mixed = mixed.astype(F32)
         squares = mean_square(mixed)
         values = (joined[:, width:] * lax.rsqrt(squares)).astype(BF)
-        moved = [
-            dot(head(values, h, size), w_hout[h * size : (h + 1) * size, :]) for h in heads
-        ]
+        moved = []
+        empty = jnp.zeros((group, size), BF)
+        for h in range(0, HEADS, 2):
+            one, two = head(values, h, size), head(values, h + 1, size)
+            both = jnp.concatenate(
+                [jnp.concatenate([one, empty], axis=1), jnp.concatenate([empty, two], axis=1)], axis=0
+            )
+            total = dot(both, w_hout[h * size : (h + 2) * size, :])
+            moved += [total[:group], total[group:]]
         pieces.append((joined[:, :width], squares * EPSILON, *moved))
     keys, floor, *moved = (jnp.concatenate(p, axis=0) for p in zip(*pieces))
 
@@ -284,10 +308,12 @@
         squares = chunk_keys * chunk_keys
         scores = [jnp.sum(head(product, h, size), axis=-1, keepdims=True) for h in heads]
         means = [jnp.mean(head(squares, h, size), axis=-1, keepdims=True) for h in heads]
-        norms = [per_edge(lax.rsqrt(m + chunk_floor)) for m in means]
-        expons = [jnp.exp2(x * n) for x, n in zip(scores, norms)]
+        norms = [per_edge(lax.rsqrt(m + chunk_floor) * scale) for m in means]
         den = edge(den_e)
-        shares = [e / (den[:, h * size : h * size + 1] + e) for h, e in enumerate(expons)]
+        shares = [
+            1.0 / (1.0 + den[:, h * size : h * size + 1] * jnp.exp2(-(x * n)))
+            for h, (x, n) in enumerate(zip(scores, norms))
+        ]
         result = edge(base_e)
         for h, share in enumerate(shares):
             result = result + share * (per_edge(take(moved[h], 2)) - edge(term_e, h))
@@ -295,10 +321,6 @@
         for e, b in enumerate(edges):
             there = pl.ds(b * levels + index * chunk, chunk)
             result_s[there, :] = result[e * chunk : (e + 1) * chunk]
-
-    copy = pltpu.make_async_copy(result_s, out_ref, sem)
-    copy.start()
-    copy.wait()
 
 
 def on_device(state, wet, w_vqkv, w_vout, w_hqkv, w_hout):
@@ -367,11 +389,7 @@
         functools.partial(halo_kernel, levels, blocks),
         out_shape=whole,
         in_specs=[vmem] * 11,
-        out_specs=hbm,
-        scratch_shapes=[
-            pltpu.VMEM(whole.shape, BF),
-            pltpu.SemaphoreType.DMA,
-        ],
+        out_specs=vmem,
         compiler_params=pltpu.CompilerParams(vmem_limit_bytes=limit),
         name="halo_blocks",
     )(from_left, from_right, *edge_values, w_vqkv, w_vout, w_hqkv, w_hout, inner)

time: 9.95 us -> 9.95 us (level)
  Pallas kernels: 6.32 us -> 6.57 us
  starting transfers between devices: 2.04 us -> 1.79 us
    pallas_call x1, Pallas kernels: 3.58 us -> 3.82 us  [on_device(): pl.pallas_call(functools.partial(early_kernel, levels), out_shape=results...]
    ppermute x1, starting transfers between devices: 1.53 us -> 1.29 us  [on_device(): lax.ppermute(to_left, 'tile', [(i, (i - 1) % tiles) for i in range(tiles)])]
  transfers between devices with their start and end apart: 2 -> 2, of which waited for: 2 -> 2; matrix products, arithmetic and copies ran while one was open for 0% -> 0% of each run, Pallas kernels for 37% -> 40%
where the time goes in v2:
time: 9.95 us; the launch traced here: 9.78 us
  Pallas kernels  6.57 us (66%)
  starting transfers between devices  1.79 us (18%)
  waiting for transfers between devices  1.32 us (13%)
    pallas_call x1, Pallas kernels, on_device(): pl.pallas_call(functools.partial(early_kernel, levels), out_shape=results...  3.82 us
    pallas_call x1, Pallas kernels, on_device(): pl.pallas_call(functools.partial(halo_kernel, levels, blocks), out_shape=...  1.86 us
    ppermute x1, starting transfers between devices, on_device(): lax.ppermute(to_left, 'tile', [(i, (i - 1) % tiles) for i in range(tiles)])  1.29 us
    ppermute x1, waiting for transfers between devices, on_device(): lax.ppermute(to_right, 'tile', [(i, (i + 1) % tiles) for i in range(tiles)])  1.14 us
    pallas_call x1, Pallas kernels, on_device(): pl.pallas_call(edge_kernel, out_shape=(one, one), in_specs=[hbm] * 2, out...  0.81 us
    ppermute x1, starting transfers between devices, on_device(): lax.ppermute(to_right, 'tile', [(i, (i + 1) % tiles) for i in range(tiles)])  0.5 us
  transfers between devices with their start and end apart: 2, of which 2 were waited for; matrix products, arithmetic and copies ran while one was open for 0% of the time, Pallas kernels for 40%

profile of v2, /device:TPU:0, one launch (start us, length us, event | category | flops | bytes accessed | tf_op | source)
XLA Modules:
  0.0 9.8 jit_solution(14633192486084604106)
XLA Ops:
  0.0 0.8 %edge_blocks.1 = (bf16[16,512]{1,0:T(8,128)(2,1)S(1)}, bf16[16,512]{1,0:T(8,128)(2,1)S(1)}) custom-call(s32[1,128]{1,0:T(1,128)} %bitcast.7, bf16[2,4,16,512]{3,2,1,0:T(8,128)(2,1)} %bitcast.4), custom_call_target="tpu_custom_call" | custom-call | flops 214748364800 | bytes 1073741824 | tf_op jit(solution)/shard_map/edge_blocks/pallas_call | solution.py:337
  0.8 0.5 %collective-permute-start = (bf16[16,512]{1,0:T(8,128)(2,1)S(1)}, bf16[16,512]{1,0:T(8,128)(2,1)S(1)}, u32[]{:S(2)}, u32[]{:S(2)}) collective-permute-start(bf16[16,512]{1,0:T(8,128)(2,1)S(1)} %get-tuple-element.18), channel_id=1, source_target_pairs={{0,1},{1,2},{2,3},{3,4},{4,5},{5,6},{6,7},{7,8},{8,9},{9,10},{10,1... | collective-permute-start | bytes 49160 | tf_op jit(solution)/shard_map/ppermute | solution.py:351
  1.3 0.0 copy-start
  1.3 0.0 copy-start.1
  1.3 0.0 copy-start.2
  1.3 0.0 copy-start.3
  1.3 0.0 copy-start.4
  1.3 0.0 copy-start.5
  1.4 3.8 %early_blocks.1 = (bf16[128,512]{1,0:T(8,128)(2,1)S(1)}, f32[64,512]{1,0:T(8,128)S(1)}, f32[64,512]{1,0:T(8,128)S(1)}, f32[4,64,512]{2,1,0:T(8,128)S(1)}, f32[64...) custom-call(bf16[128,512]{1,0:T(8,128)(2,1)} %bitcast.5, bf16[512,1536]{1,0:T(8,128)(2,1)} %w_vqkv.1, ...), custom_call_target="tpu_custom_call" | custom-call | flops 536870912 | bytes 8388608 | tf_op jit(solution)/shard_map/early_blocks/pallas_call | solution.py:367
  5.2 1.3 %collective-permute-start.1 = (bf16[16,512]{1,0:T(8,128)(2,1)S(1)}, bf16[16,512]{1,0:T(8,128)(2,1)S(1)}, u32[]{:S(2)}, u32[]{:S(2)}) collective-permute-start(bf16[16,512]{1,0:T(8,128)(2,1)S(1)} %get-tuple-element.20), channel_id=1, source_target_pairs={{0,15},{1,0},{2,1},{3,2},{4,3},{5,4},{6,5},{7,6},{8,7},{9,8},{10,9... | collective-permute-start | bytes 49160 | tf_op jit(solution)/shard_map/ppermute | solution.py:376
  6.5 0.0 copy-done
  6.5 0.0 copy-done.1
  6.5 0.0 copy-done.2
  6.5 0.0 copy-done.3
  6.5 0.0 copy-done.4
  6.5 0.0 copy-done.5
  6.5 0.1 late_blocks.1
  6.6 1.1 %collective-permute-done.from_left = bf16[16,512]{1,0:T(8,128)(2,1)S(1)} collective-permute-done((bf16[16,512]{1,0:T(8,128)(2,1)S(1)}, bf16[16,512]{1,0:T(8,128)(2,1)S(1)}, u32[]{:S(2)}, u32[]{:S(2)}) %collective-permute-start) | collective-permute-done | bytes 16416 | tf_op jit(solution)/shard_map/ppermute | solution.py:351
  7.7 0.2 %collective-permute-done.1.from_right = bf16[16,512]{1,0:T(8,128)(2,1)S(1)} collective-permute-done((bf16[16,512]{1,0:T(8,128)(2,1)S(1)}, bf16[16,512]{1,0:T(8,128)(2,1)S(1)}, u32[]{:S(2)}, u32[]{:S(2)}) %collective-permute-start.1) | collective-permute-done | bytes 16416 | tf_op jit(solution)/shard_map/ppermute | solution.py:376
  7.9 1.9 %halo_blocks.1 = bf16[128,512]{1,0:T(8,128)(2,1)} custom-call(bf16[16,512]{1,0:T(8,128)(2,1)S(1)} %collective-permute-done.from_left, bf16[16,512]{1,0:T(8,128)(2,1)S(1)} %collective-permute-done.1.from_right, f32[64,512]{1,0:T(8,128)S(1)} %get-tuple-element.26.base_e, f32[64,512]{1,0:T(8,128)S(1)} %get-tuple-element.27.query_e, ...), custom_call_target="tpu_custom_call" | custom-call | tf_op jit(solution)/shard_map/halo_blocks/pallas_call | solution.py:388
Async XLA Ops:
  0.8 6.9 %collective-permute-start = (bf16[16,512]{1,0:T(8,128)(2,1)S(1)}, bf16[16,512]{1,0:T(8,128)(2,1)S(1)}, u32[]{:S(2)}, u32[]{:S(2)}) collective-permute-start(bf16[16,512]{1,0:T(8,128)(2,1)S(1)} %get-tuple-element.18), channel_id=1, source_target_pairs={{0,1},{1,2},{2,3},{3,4},{4,5},{5,6},{6,7},{7,8},{8,9},{9,10},{10,1... | collective-permute-start | bytes 49160 | tf_op jit(solution)/shard_map/ppermute | solution.py:351
  1.3 5.2 %copy-start = (bf16[512,1536]{1,0:T(8,128)(2,1)S(1)}, bf16[512,1536]{1,0:T(8,128)(2,1)}, u32[]{:S(2)}) copy-start(bf16[512,1536]{1,0:T(8,128)(2,1)} %w_vqkv.1) | copy-start | bytes 4718596
  1.3 5.2 %copy-start.1 = (bf16[512,1536]{1,0:T(8,128)(2,1)S(1)}, bf16[512,1536]{1,0:T(8,128)(2,1)}, u32[]{:S(2)}) copy-start(bf16[512,1536]{1,0:T(8,128)(2,1)} %w_hqkv.1) | copy-start | bytes 4718596
  1.3 5.2 %copy-start.2 = (bf16[512,512]{1,0:T(8,128)(2,1)S(1)}, bf16[512,512]{1,0:T(8,128)(2,1)}, u32[]{:S(2)}) copy-start(bf16[512,512]{1,0:T(8,128)(2,1)} %w_vout.1) | copy-start | bytes 1572868
  1.3 5.2 %copy-start.3 = (bf16[512,512]{1,0:T(8,128)(2,1)S(1)}, bf16[512,512]{1,0:T(8,128)(2,1)}, u32[]{:S(2)}) copy-start(bf16[512,512]{1,0:T(8,128)(2,1)} %w_hout.1) | copy-start | bytes 1572868
  1.3 5.2 %copy-start.4 = (bf16[8,16,512]{2,1,0:T(8,128)(2,1)S(1)}, bf16[8,16,512]{2,1,0:T(8,128)(2,1)}, u32[]{:S(2)}) copy-start(bf16[8,16,512]{2,1,0:T(8,128)(2,1)} %param.6) | copy-start | bytes 393220
  1.3 5.2 %copy-start.5 = (s32[128]{0:T(128)S(1)}, s32[128]{0:T(128)}, u32[]{:S(2)}) copy-start(s32[128]{0:T(128)} %param.7) | copy-start | bytes 1540
  5.2 2.7 %collective-permute-start.1 = (bf16[16,512]{1,0:T(8,128)(2,1)S(1)}, bf16[16,512]{1,0:T(8,128)(2,1)S(1)}, u32[]{:S(2)}, u32[]{:S(2)}) collective-permute-start(bf16[16,512]{1,0:T(8,128)(2,1)S(1)} %get-tuple-element.20), channel_id=1, source_target_pairs={{0,15},{1,0},{2,1},{3,2},{4,3},{5,4},{6,5},{7,6},{8,7},{9,8},{10,9... | collective-permute-start | bytes 49160 | tf_op jit(solution)/shard_map/ppermute | solution.py:376
